TPU v7x, 32 devices: a whole 2x2x4 slice. The times are simulated.
32 devices in a mesh: seq: 8 (over z, x), batch: 4 (over y, core).
Axes of the slice: x: 2, y: 2, z: 4, core: 2. Of those that a mesh axis runs over, the one named last changes fastest.
Arguments:
- inputs: bfloat16 [4, 1024, 768], P('batch', 'seq'), may hold values from -6 to 6
- cotangent: bfloat16 [4, 1024, 768], P('batch', 'seq'), may hold values from -6 to 6
- doc_lengths: int32 [4, 9], P('batch'), may hold values from 1 to 896, as said below
- gain_one: float32 [768], replicated, may hold values from 0.5 to 1.5
- shift_one: float32 [768], replicated, may hold values from -2 to 2
- qkv_weight: bfloat16 [768, 2304], replicated, may hold values from -0.21875 to 0.21875
- qkv_bias: float32 [2304], replicated, may hold values from -2 to 2
- proj_weight: bfloat16 [768, 768], replicated, may hold values from -6 to 6
- proj_bias: float32 [768], replicated, may hold values from -2 to 2
- gain_two: float32 [768], replicated, may hold values from 0.5 to 1.5
- shift_two: float32 [768], replicated, may hold values from -2 to 2
- up_weight: bfloat16 [768, 3072], replicated, may hold values from -0.21875 to 0.21875
- up_bias: float32 [3072], replicated, may hold values from -2 to 2
- down_weight: bfloat16 [3072, 768], replicated, may hold values from -0.109375 to 0.109375
- down_bias: float32 [768], replicated, may hold values from -2 to 2
Outputs:
- layer_out: bfloat16 [4, 1024, 768], P('batch', 'seq')
- input_grad: bfloat16 [4, 1024, 768], P('batch', 'seq')
- grad_gain_one: float32 [768], replicated
- grad_shift_one: float32 [768], replicated
- grad_qkv_weight: float32 [768, 2304], replicated
- grad_qkv_bias: float32 [2304], replicated
- grad_proj_weight: float32 [768, 768], replicated
- grad_proj_bias: float32 [768], replicated
- grad_gain_two: float32 [768], replicated
- grad_shift_two: float32 [768], replicated
- grad_up_weight: float32 [768, 3072], replicated
- grad_up_bias: float32 [3072], replicated
- grad_down_weight: float32 [3072, 768], replicated
- grad_down_bias: float32 [768], replicated
Inputs may be any that keep to these rules, and one draw needn't show every extreme that they name: `doc_lengths`: each row lists in order the lengths of the 9 documents packed into one stream: 8 short ones that hold 128 tokens together, and one of exactly 896 tokens with at least one short document before it and one after it.
All inputs are finite; a program needn't handle non-finite values.
Results may differ from a plain program's by a relative error of at most 0.018.
Values may be sent and summed in bfloat16 or wider, within the bound.
A program may use at most 256 MiB of HBM per device.

v0:
```python
import math
import jax
import jax.numpy as jnp
from jax import lax
from jax.sharding import PartitionSpec as P

HEADS = 12
HD = 64
norm_eps = 1e-05
masked_low = -1e30


def from_behind(shard, axis, by):
    peers = lax.axis_size(axis)
    pairs = [(i, i + by) for i in range(peers) if 0 <= i + by < peers]
    return lax.ppermute(shard, axis, pairs)


def shifted(block, axis, distance):
    devices = range(lax.axis_size(axis))
    route = [((i - distance) % len(devices), i) for i in devices]
    return lax.ppermute(block, axis, route)


def layer_norm(rows, gain, shift):
    center = rows - jnp.mean(rows, axis=-1, keepdims=True)
    spread = jnp.mean(center * center, axis=-1, keepdims=True)
    return center * lax.rsqrt(spread + norm_eps) * gain + shift


def gelu_tanh(value):
    return jax.nn.gelu(value, approximate=True)


def doc_of(ends, first, count):
    places = first + jnp.arange(count, dtype=jnp.int32)
    return jnp.sum((ends[None, :] <= places[:, None]).astype(jnp.int32), axis=1)


def scores_of(q_heads, k_heads, allowed):
    raw = jnp.einsum("qhd,khd->hqk", q_heads, k_heads, preferred_element_type=jnp.float32)
    return jnp.where(allowed[None], raw * (1.0 / math.sqrt(q_heads.shape[2])), 0.0)


def forward_part(state, q_heads, k_heads, v_heads, allowed):
    running, total, accum = state
    scores = scores_of(q_heads, k_heads, allowed)
    top = jnp.max(jnp.where(allowed[None], jnp.abs(scores), masked_low), axis=2)
    newer = jnp.maximum(running, top)
    plus = jnp.where(allowed[None], jnp.exp(scores - newer[:, :, None]), 0.0)
    minus = jnp.where(allowed[None], jnp.exp(-scores - newer[:, :, None]), 0.0)
    keep = jnp.exp(running - newer)
    total = total * keep + jnp.sum(plus + minus, axis=2)
    weights = (plus - minus).astype(jnp.bfloat16)
    accum = accum * keep[:, :, None] + jnp.einsum(
        "hqk,khd->hqd", weights, v_heads, preferred_element_type=jnp.float32
    )
    return (newer, total, accum)


def backward_part(q_heads, k_heads, v_heads, grad_out, log_total, delta, allowed):
    scale = 1.0 / math.sqrt(q_heads.shape[2])
    scores = scores_of(q_heads, k_heads, allowed)
    plus = jnp.where(allowed[None], jnp.exp(scores - log_total[:, :, None]), 0.0)
    minus = jnp.where(allowed[None], jnp.exp(-scores - log_total[:, :, None]), 0.0)
    signed = plus - minus
    along = jnp.einsum("qhd,khd->hqk", grad_out, v_heads, preferred_element_type=jnp.float32)
    dscore = (((plus + minus) * along - signed * delta[:, :, None]) * scale).astype(jnp.bfloat16)
    weights = signed.astype(jnp.bfloat16)
    grad_q = jnp.einsum("hqk,khd->qhd", dscore, k_heads, preferred_element_type=jnp.float32)
    grad_k = jnp.einsum("hqk,qhd->khd", dscore, q_heads, preferred_element_type=jnp.float32)
    grad_v = jnp.einsum("hqk,qhd->khd", weights, grad_out, preferred_element_type=jnp.float32)
    return (grad_q, grad_k, grad_v)


def forward_step(state, q_heads, k_heads, v_heads, allowed):
    return forward_part(state, q_heads, k_heads, v_heads, allowed)


def backward_step(q_heads, k_heads, v_heads, grad_out, log_total, delta, allowed):
    return backward_part(q_heads, k_heads, v_heads, grad_out, log_total, delta, allowed)


def per_device(
    inputs,
    cotangent,
    doc_lengths,
    gain_one,
    shift_one,
    qkv_weight,
    qkv_bias,
    proj_weight,
    proj_bias,
    gain_two,
    shift_two,
    up_weight,
    up_bias,
    down_weight,
    down_bias,
):
    rows = inputs.shape[1]
    width = inputs.shape[2]
    index = lax.axis_index("seq")
    count = lax.axis_size("seq")
    ends = jnp.cumsum(doc_lengths[0])
    q_place = index * rows + jnp.arange(rows, dtype=jnp.int32)
    q_doc = doc_of(ends, index * rows, rows)

    def heads(flat):
        return flat.reshape(flat.shape[0], HEADS, HD)

    x_rows = inputs[0].astype(jnp.float32)
    norm_one = layer_norm(x_rows, gain_one, shift_one).astype(jnp.bfloat16)
    mixed = (jnp.dot(norm_one, qkv_weight, preferred_element_type=jnp.float32) + qkv_bias).astype(
        jnp.bfloat16
    )
    q_flat = mixed[:, :width]
    k_flat = mixed[:, width : 2 * width]
    v_flat = mixed[:, 2 * width :]
    q_heads = heads(q_flat)

    def allowed_for(first, extent):
        k_place = first + jnp.arange(extent, dtype=jnp.int32)
        k_doc = doc_of(ends, first, extent)
        return (q_doc[:, None] == k_doc[None, :]) & (k_place[None, :] <= q_place[:, None])

    start_state = (
        jnp.full((HEADS, rows), masked_low, jnp.float32),
        jnp.zeros((HEADS, rows), jnp.float32),
        jnp.zeros((HEADS, rows, HD), jnp.float32),
    )
    state = start_state
    k_all = lax.all_gather(k_flat, "seq", axis=0, tiled=True)
    v_all = lax.all_gather(v_flat, "seq", axis=0, tiled=True)
    fold_extent = k_all.shape[0]
    number = fold_extent // rows

    def one(inner, block):
        offset = block * rows
        k_blk = lax.dynamic_slice_in_dim(k_all, offset, rows, 0)
        v_blk = lax.dynamic_slice_in_dim(v_all, offset, rows, 0)
        allowed = allowed_for(offset, rows)
        return (forward_step(inner, q_heads, heads(k_blk), heads(v_blk), allowed), None)

    state, unused = lax.scan(one, state, jnp.arange(number, dtype=jnp.int32))
    running, total, accum = state
    attn_heads = accum / total[:, :, None]
    attn32 = jnp.transpose(attn_heads, (1, 0, 2)).reshape(rows, width)
    attn = attn32.astype(jnp.bfloat16)
    resid = x_rows + jnp.dot(attn, proj_weight, preferred_element_type=jnp.float32) + proj_bias
    norm_two = layer_norm(resid, gain_two, shift_two).astype(jnp.bfloat16)
    hidden = jnp.dot(norm_two, up_weight, preferred_element_type=jnp.float32) + up_bias
    active = gelu_tanh(hidden).astype(jnp.bfloat16)
    result = resid + jnp.dot(active, down_weight, preferred_element_type=jnp.float32) + down_bias
    layer_out = result.astype(jnp.bfloat16)[None]
    grad_rows = cotangent[0]
    grad_down_weight = jnp.einsum(
        "tf,td->fd", active, grad_rows, preferred_element_type=jnp.float32
    )
    grad_down_bias = jnp.sum(grad_rows.astype(jnp.float32), axis=0)
    grad_active = jnp.dot(grad_rows, down_weight.T, preferred_element_type=jnp.float32)
    gelu_back = jax.vjp(gelu_tanh, hidden)[1]
    grad_hidden = gelu_back(grad_active)[0].astype(jnp.bfloat16)
    grad_up_weight = jnp.einsum(
        "td,tf->df", norm_two, grad_hidden, preferred_element_type=jnp.float32
    )
    grad_up_bias = jnp.sum(grad_hidden.astype(jnp.float32), axis=0)
    grad_norm_two = jnp.dot(grad_hidden, up_weight.T, preferred_element_type=jnp.float32)
    norm_two_back = jax.vjp(layer_norm, resid, gain_two, shift_two)[1]
    resid_part, grad_gain_two, grad_shift_two = norm_two_back(grad_norm_two)
    grad_resid = grad_rows.astype(jnp.float32) + resid_part
    grad_branch = grad_resid.astype(jnp.bfloat16)
    grad_proj_weight = jnp.einsum(
        "td,te->de", attn, grad_branch, preferred_element_type=jnp.float32
    )
    grad_proj_bias = jnp.sum(grad_branch.astype(jnp.float32), axis=0)
    grad_attn = jnp.dot(grad_branch, proj_weight.T, preferred_element_type=jnp.float32).astype(
        jnp.bfloat16
    )
    grad_out = heads(grad_attn)
    log_total = running + jnp.log(total)
    delta = jnp.einsum("qhd,hqd->hq", grad_out.astype(jnp.float32), attn_heads)

    def circle_step(step, carry):
        k_held, v_held, acc_k, acc_v, grad_q = carry
        source = jnp.remainder(index - step, count)
        allowed = allowed_for(source * rows, rows)
        part = backward_step(
            q_heads, heads(k_held), heads(v_held), grad_out, log_total, delta, allowed
        )
        grad_q = grad_q + part[0]
        acc_k = acc_k + part[1].reshape(rows, width)
        acc_v = acc_v + part[2].reshape(rows, width)
        k_held, v_held = from_behind((k_held, v_held), "seq", 1)
        acc_k, acc_v = (
            shifted(acc_k.astype(jnp.bfloat16), "seq", 1).astype(acc_k.dtype),
            shifted(acc_v.astype(jnp.bfloat16), "seq", 1).astype(acc_v.dtype),
        )
        return (k_held, v_held, acc_k, acc_v, grad_q)

    circle_start = (
        k_flat,
        v_flat,
        jnp.zeros((rows, width), jnp.float32),
        jnp.zeros((rows, width), jnp.float32),
        jnp.zeros((rows, HEADS, HD), jnp.float32),
    )
    unused_k, unused_v, grad_k, grad_v, grad_q = lax.fori_loop(0, count, circle_step, circle_start)
    grad_mixed = jnp.concatenate(
        [
            grad_q.reshape(rows, width).astype(jnp.bfloat16),
            grad_k.astype(jnp.bfloat16),
            grad_v.astype(jnp.bfloat16),
        ],
        axis=1,
    )
    grad_qkv_weight = jnp.einsum(
        "td,te->de", norm_one, grad_mixed, preferred_element_type=jnp.float32
    )
    grad_qkv_bias = jnp.sum(grad_mixed.astype(jnp.float32), axis=0)
    grad_norm_one = jnp.dot(grad_mixed, qkv_weight.T, preferred_element_type=jnp.float32)
    norm_one_back = jax.vjp(layer_norm, x_rows, gain_one, shift_one)[1]
    input_part, grad_gain_one, grad_shift_one = norm_one_back(grad_norm_one)
    input_grad = (grad_resid + input_part).astype(jnp.bfloat16)[None]
    members = (
        grad_gain_one,
        grad_shift_one,
        grad_qkv_weight,
        grad_qkv_bias,
        grad_proj_weight,
        grad_proj_bias,
        grad_gain_two,
        grad_shift_two,
        grad_up_weight,
        grad_up_bias,
        grad_down_weight,
        grad_down_bias,
    )
    joined = jnp.concatenate([member.reshape(-1) for member in members])
    summed = lax.psum_scatter(joined, ("seq", "batch"), scatter_dimension=0, tiled=True)
    whole = lax.all_gather(
        summed.astype(jnp.bfloat16), ("seq", "batch"), axis=0, tiled=True
    ).astype(summed.dtype)
    outputs = []
    offset = 0
    for member in members:
        extent = member.size
        outputs.append(whole[offset : offset + extent].reshape(member.shape))
        offset = offset + extent
    return (
        layer_out,
        input_grad,
        outputs[0],
        outputs[1],
        outputs[2],
        outputs[3],
        outputs[4],
        outputs[5],
        outputs[6],
        outputs[7],
        outputs[8],
        outputs[9],
        outputs[10],
        outputs[11],
    )


def solution(mesh):
    in_specs = (
        P("batch", "seq", None),
        P("batch", "seq", None),
        P("batch", None),
        P(),
        P(),
        P(),
        P(),
        P(),
        P(),
        P(),
        P(),
        P(),
        P(),
        P(),
        P(),
    )
    out_specs = (
        P("batch", "seq", None),
        P("batch", "seq", None),
        P(),
        P(),
        P(),
        P(),
        P(),
        P(),
        P(),
        P(),
        P(),
        P(),
        P(),
        P(),
    )
    return jax.shard_map(
        per_device, mesh=mesh, in_specs=in_specs, out_specs=out_specs, check_vma=False
    )
```

profile of v0, /device:TPU:0, one launch (start us, length us, event | category | flops | bytes accessed | tf_op | source)
XLA Modules:
  0.0 1429.9 jit_solution(15000022725188257302)
XLA Ops:
  20.7 38.8 %all-gather.3.cloned.1.call-done = bf16[1024,768]{1,0:T(8,128)(2,1)} async-done(((bf16[128,768]{1,0:T(8,128)(2,1)}), bf16[1024,768]{1,0:T(8,128)(2,1)}) %all-gather.3.cloned.1.call-update) | async-done | bytes 1572880 | tf_op jit(solution)/shard_map/all_gather | solution.py:133
  59.4 45.8 %all-gather.5.cloned.1.call-done = bf16[1024,768]{1,0:T(8,128)(2,1)} async-done(((bf16[128,768]{1,0:T(8,128)(2,1)}), bf16[1024,768]{1,0:T(8,128)(2,1)}) %all-gather.5.cloned.1.call-update) | async-done | bytes 1572880 | tf_op jit(solution)/shard_map/all_gather | solution.py:134
  105.7 144.0 %while.39 = (s32[]{:T(128)}, f32[12,128]{1,0:T(8,128)}, f32[12,128]{1,0:T(8,128)}, f32[12,128,64]{1,2,0:T(8,128)}, s32[128]{0:T(128)}, /*index=5*/s32[9]{0:T(128...) while((s32[]{:T(128)}, f32[12,128]{1,0:T(8,128)}, ...), condition=%wide.region_8.9_spmd.clone, body=%wide.region_4.8_spmd.clone.sunk | while | flops 54422532 | bytes 5542175 | solution.py:145
  112.7 2.9 select_reduce_fusion.2
  129.9 2.9 select_reduce_fusion.2
  148.0 2.9 select_reduce_fusion.2
  166.1 2.9 select_reduce_fusion.2
  184.2 2.9 select_reduce_fusion.2
  202.3 2.9 select_reduce_fusion.2
  220.4 2.9 select_reduce_fusion.2
  238.6 2.9 select_reduce_fusion.2
  253.0 3.3 convolution_add_fusion.2
  256.4 5.5 convert_reduce_fusion.2
  272.0 215.4 %while.40 = (s32[]{:T(128)}, bf16[128,768]{0,1:T(8,128)(2,1)}, bf16[128,768]{0,1:T(8,128)(2,1)}, f32[128,768]{0,1:T(8,128)}, f32[128,768]{0,1:T(8,128)}, /*index...) while((s32[]{:T(128)}, bf16[128,768]{0,1:T(8,128)(2,1)}, ...), condition=%wide.region_15.16_spmd.clone, body=%wide.region_13.15_spmd.clone.sunk | while | flops 130993680 | bytes 19995340 | solution.py:208
  273.6 3.1 collective-permute-start
  278.3 4.7 collective-permute-start.1
  293.7 5.5 collective-permute-done.2
  321.9 3.9 collective-permute-done.2
  334.8 3.0 collective-permute-start.1
  347.6 4.5 collective-permute-done.2
  386.5 3.6 collective-permute-start.1
  397.0 2.8 collective-permute-start.3
  413.4 3.6 collective-permute-start.1
  427.4 3.9 collective-permute-done.2
  465.6 3.6 collective-permute-start.1
  476.1 2.8 collective-permute-start.3
  493.2 4.2 fusion.60
  499.6 5.3 convolution_bitcast_fusion.1
  504.8 5.2 fusion.51
  510.6 7.9 reshape.357
  520.9 9.6 copy.69
  530.5 10.8 reshape.360
  547.7 60.7 %dynamic-update-slice.3 = f32[7087872]{0:T(1024)} dynamic-update-slice(f32[7087872]{0:T(1024)} %constant_dynamic-update-slice_fusion.8, f32[1769472]{0:T(1024)} %reshape.357, s32[]{} %constant.149) | dynamic-update-slice | bytes 14155780
  609.7 20.3 %dynamic-update-slice.5 = f32[7087872]{0:T(1024)} dynamic-update-slice(f32[7087872]{0:T(1024)} %constant_dynamic-update-slice_fusion.7, f32[589824]{0:T(1024)S(1)} %reshape.358, s32[]{} %constant.151) | dynamic-update-slice | bytes 4718596
  633.9 9.3 constant_dynamic-update-slice_fusion.3
  643.8 3.9 constant_dynamic-update-slice_fusion.1
  648.4 457.8 %all-reduce.6 = bf16[7087872]{0:T(1024)(128)(2,1)} all-reduce(f32[7087872]{0:T(1024)} %constant_dynamic-update-slice_fusion), channel_id=2, replica_groups=mesh['seq'=8,'batch'=4] {'seq','batch'}, use_global_device_ids=true, to_apply=%region_26.27.clone | all-reduce | flops 7087872 | bytes 42527232
  1107.4 5.2 broadcast.252
  1112.7 7.6 dynamic-update-slice
  1121.6 4.1 fusion.35
  1125.7 242.6 %all-reduce.5.cloned.1.call-done = bf16[7087872]{0:T(1024)(128)(2,1)} async-done(((bf16[7087872]{0:T(1024)(128)(2,1)}), bf16[7087872]{0:T(1024)(128)(2,1)}) %all-reduce.5.cloned.1.call-update) | async-done | bytes 14175760
  1368.3 9.6 fusion.69
  1377.9 10.9 reshape.362
  1388.8 11.3 slice.80
  1400.1 4.7 slice.87
  1404.7 8.2 reshape.361
  1413.0 3.0 slice.89
  1416.0 3.4 slice.73
  (567 shorter events, 342.4 us)
Async XLA Ops:
  7.2 52.3 %all-gather.3.cloned.1.call-start = ((), (), s32[]{:S(2)}) async-start(), calls=%async_computation | async-start | bytes 1769472 | tf_op jit(solution)/shard_map/all_gather | solution.py:133
  12.6 92.6 %all-gather.5.cloned.1.call-start = ((), (), s32[]{:S(2)}) async-start(), calls=%async_computation.1 | async-start | bytes 1769472 | tf_op jit(solution)/shard_map/all_gather | solution.py:134
  13.4 1354.9 %all-reduce.5.cloned.1.call-start = ((), (), s32[]{:S(2)}) async-start(), calls=%async_computation.2 | async-start | bytes 28352512
  252.7 11.5 copy-start.4
  272.0 13.9 copy-start.48
  272.0 13.9 copy-start.49
  273.6 29.4 %collective-permute-start = (bf16[128,768]{0,1:T(8,128)(2,1)}, bf16[128,768]{0,1:T(8,128)(2,1)}, u32[]{:S(2)}, u32[]{:S(2)}) collective-permute-start(bf16[128,768]{0,1:T(8,128)(2,1)} %copy.93), channel_id=1, source_target_pairs={{0,4},{4,8},{8,12},{12,16},{16,20},{20,24},{24,28},{1,5},{5,9},{9,... | collective-permute-start | bytes 589832 | tf_op jit(solution)/shard_map/while/body/eval_jaxpr/ppermute | solution.py:16
  278.3 24.7 %collective-permute-start.1 = (bf16[128,768]{0,1:T(8,128)(2,1)}, bf16[128,768]{0,1:T(8,128)(2,1)}, u32[]{:S(2)}, u32[]{:S(2)}) collective-permute-start(bf16[128,768]{0,1:T(8,128)(2,1)} %copy.94), channel_id=1, source_target_pairs={{0,4},{4,8},{8,12},{12,16},{16,20},{20,24},{24,28},{1,5},{5,9},{9,... | collective-permute-start | bytes 589832 | tf_op jit(solution)/shard_map/while/body/eval_jaxpr/ppermute | solution.py:16
  288.7 10.5 collective-permute-start.2
  290.0 11.3 collective-permute-start.3
  304.7 24.9 %collective-permute-start = (bf16[128,768]{0,1:T(8,128)(2,1)}, bf16[128,768]{0,1:T(8,128)(2,1)}, u32[]{:S(2)}, u32[]{:S(2)}) collective-permute-start(bf16[128,768]{0,1:T(8,128)(2,1)} %copy.93), channel_id=1, source_target_pairs={{0,4},{4,8},{8,12},{12,16},{16,20},{20,24},{24,28},{1,5},{5,9},{9,... | collective-permute-start | bytes 589832 | tf_op jit(solution)/shard_map/while/body/eval_jaxpr/ppermute | solution.py:16
  308.2 21.4 %collective-permute-start.1 = (bf16[128,768]{0,1:T(8,128)(2,1)}, bf16[128,768]{0,1:T(8,128)(2,1)}, u32[]{:S(2)}, u32[]{:S(2)}) collective-permute-start(bf16[128,768]{0,1:T(8,128)(2,1)} %copy.94), channel_id=1, source_target_pairs={{0,4},{4,8},{8,12},{12,16},{16,20},{20,24},{24,28},{1,5},{5,9},{9,... | collective-permute-start | bytes 589832 | tf_op jit(solution)/shard_map/while/body/eval_jaxpr/ppermute | solution.py:16
  316.5 9.3 collective-permute-start.2
  317.8 10.1 collective-permute-start.3
  331.2 24.7 %collective-permute-start = (bf16[128,768]{0,1:T(8,128)(2,1)}, bf16[128,768]{0,1:T(8,128)(2,1)}, u32[]{:S(2)}, u32[]{:S(2)}) collective-permute-start(bf16[128,768]{0,1:T(8,128)(2,1)} %copy.93), channel_id=1, source_target_pairs={{0,4},{4,8},{8,12},{12,16},{16,20},{20,24},{24,28},{1,5},{5,9},{9,... | collective-permute-start | bytes 589832 | tf_op jit(solution)/shard_map/while/body/eval_jaxpr/ppermute | solution.py:16
  334.8 21.1 %collective-permute-start.1 = (bf16[128,768]{0,1:T(8,128)(2,1)}, bf16[128,768]{0,1:T(8,128)(2,1)}, u32[]{:S(2)}, u32[]{:S(2)}) collective-permute-start(bf16[128,768]{0,1:T(8,128)(2,1)} %copy.94), channel_id=1, source_target_pairs={{0,4},{4,8},{8,12},{12,16},{16,20},{20,24},{24,28},{1,5},{5,9},{9,... | collective-permute-start | bytes 589832 | tf_op jit(solution)/shard_map/while/body/eval_jaxpr/ppermute | solution.py:16
  343.4 8.7 collective-permute-start.2
  344.8 9.5 collective-permute-start.3
  357.6 23.7 %collective-permute-start = (bf16[128,768]{0,1:T(8,128)(2,1)}, bf16[128,768]{0,1:T(8,128)(2,1)}, u32[]{:S(2)}, u32[]{:S(2)}) collective-permute-start(bf16[128,768]{0,1:T(8,128)(2,1)} %copy.93), channel_id=1, source_target_pairs={{0,4},{4,8},{8,12},{12,16},{16,20},{20,24},{24,28},{1,5},{5,9},{9,... | collective-permute-start | bytes 589832 | tf_op jit(solution)/shard_map/while/body/eval_jaxpr/ppermute | solution.py:16
  361.1 20.1 %collective-permute-start.1 = (bf16[128,768]{0,1:T(8,128)(2,1)}, bf16[128,768]{0,1:T(8,128)(2,1)}, u32[]{:S(2)}, u32[]{:S(2)}) collective-permute-start(bf16[128,768]{0,1:T(8,128)(2,1)} %copy.94), channel_id=1, source_target_pairs={{0,4},{4,8},{8,12},{12,16},{16,20},{20,24},{24,28},{1,5},{5,9},{9,... | collective-permute-start | bytes 589832 | tf_op jit(solution)/shard_map/while/body/eval_jaxpr/ppermute | solution.py:16
  368.7 8.7 collective-permute-start.2
  370.1 9.5 collective-permute-start.3
  381.2 11.6 copy-start.48
  381.2 11.6 copy-start.49
  382.9 25.3 %collective-permute-start = (bf16[128,768]{0,1:T(8,128)(2,1)}, bf16[128,768]{0,1:T(8,128)(2,1)}, u32[]{:S(2)}, u32[]{:S(2)}) collective-permute-start(bf16[128,768]{0,1:T(8,128)(2,1)} %copy.93), channel_id=1, source_target_pairs={{0,4},{4,8},{8,12},{12,16},{16,20},{20,24},{24,28},{1,5},{5,9},{9,... | collective-permute-start | bytes 589832 | tf_op jit(solution)/shard_map/while/body/eval_jaxpr/ppermute | solution.py:16
  386.5 21.7 %collective-permute-start.1 = (bf16[128,768]{0,1:T(8,128)(2,1)}, bf16[128,768]{0,1:T(8,128)(2,1)}, u32[]{:S(2)}, u32[]{:S(2)}) collective-permute-start(bf16[128,768]{0,1:T(8,128)(2,1)} %copy.94), channel_id=1, source_target_pairs={{0,4},{4,8},{8,12},{12,16},{16,20},{20,24},{24,28},{1,5},{5,9},{9,... | collective-permute-start | bytes 589832 | tf_op jit(solution)/shard_map/while/body/eval_jaxpr/ppermute | solution.py:16
  395.6 8.7 collective-permute-start.2
  397.0 9.5 collective-permute-start.3
  408.1 11.7 copy-start.48
  408.1 11.7 copy-start.49
  409.8 25.3 %collective-permute-start = (bf16[128,768]{0,1:T(8,128)(2,1)}, bf16[128,768]{0,1:T(8,128)(2,1)}, u32[]{:S(2)}, u32[]{:S(2)}) collective-permute-start(bf16[128,768]{0,1:T(8,128)(2,1)} %copy.93), channel_id=1, source_target_pairs={{0,4},{4,8},{8,12},{12,16},{16,20},{20,24},{24,28},{1,5},{5,9},{9,... | collective-permute-start | bytes 589832 | tf_op jit(solution)/shard_map/while/body/eval_jaxpr/ppermute | solution.py:16
  413.4 21.7 %collective-permute-start.1 = (bf16[128,768]{0,1:T(8,128)(2,1)}, bf16[128,768]{0,1:T(8,128)(2,1)}, u32[]{:S(2)}, u32[]{:S(2)}) collective-permute-start(bf16[128,768]{0,1:T(8,128)(2,1)} %copy.94), channel_id=1, source_target_pairs={{0,4},{4,8},{8,12},{12,16},{16,20},{20,24},{24,28},{1,5},{5,9},{9,... | collective-permute-start | bytes 589832 | tf_op jit(solution)/shard_map/while/body/eval_jaxpr/ppermute | solution.py:16
  422.6 8.7 collective-permute-start.2
  423.9 9.5 collective-permute-start.3
  436.7 23.7 %collective-permute-start = (bf16[128,768]{0,1:T(8,128)(2,1)}, bf16[128,768]{0,1:T(8,128)(2,1)}, u32[]{:S(2)}, u32[]{:S(2)}) collective-permute-start(bf16[128,768]{0,1:T(8,128)(2,1)} %copy.93), channel_id=1, source_target_pairs={{0,4},{4,8},{8,12},{12,16},{16,20},{20,24},{24,28},{1,5},{5,9},{9,... | collective-permute-start | bytes 589832 | tf_op jit(solution)/shard_map/while/body/eval_jaxpr/ppermute | solution.py:16
  440.3 20.1 %collective-permute-start.1 = (bf16[128,768]{0,1:T(8,128)(2,1)}, bf16[128,768]{0,1:T(8,128)(2,1)}, u32[]{:S(2)}, u32[]{:S(2)}) collective-permute-start(bf16[128,768]{0,1:T(8,128)(2,1)} %copy.94), channel_id=1, source_target_pairs={{0,4},{4,8},{8,12},{12,16},{16,20},{20,24},{24,28},{1,5},{5,9},{9,... | collective-permute-start | bytes 589832 | tf_op jit(solution)/shard_map/while/body/eval_jaxpr/ppermute | solution.py:16
  447.9 8.7 collective-permute-start.2
  449.2 9.5 collective-permute-start.3
  460.4 11.6 copy-start.48
  460.4 11.6 copy-start.49
  462.0 25.3 %collective-permute-start = (bf16[128,768]{0,1:T(8,128)(2,1)}, bf16[128,768]{0,1:T(8,128)(2,1)}, u32[]{:S(2)}, u32[]{:S(2)}) collective-permute-start(bf16[128,768]{0,1:T(8,128)(2,1)} %copy.93), channel_id=1, source_target_pairs={{0,4},{4,8},{8,12},{12,16},{16,20},{20,24},{24,28},{1,5},{5,9},{9,... | collective-permute-start | bytes 589832 | tf_op jit(solution)/shard_map/while/body/eval_jaxpr/ppermute | solution.py:16
  465.6 21.7 %collective-permute-start.1 = (bf16[128,768]{0,1:T(8,128)(2,1)}, bf16[128,768]{0,1:T(8,128)(2,1)}, u32[]{:S(2)}, u32[]{:S(2)}) collective-permute-start(bf16[128,768]{0,1:T(8,128)(2,1)} %copy.94), channel_id=1, source_target_pairs={{0,4},{4,8},{8,12},{12,16},{16,20},{20,24},{24,28},{1,5},{5,9},{9,... | collective-permute-start | bytes 589832 | tf_op jit(solution)/shard_map/while/body/eval_jaxpr/ppermute | solution.py:16
  474.8 8.7 collective-permute-start.2
  476.1 9.5 collective-permute-start.3
  530.5 12.1 copy-start.15
  609.7 20.3 %copy-start.40 = (f32[768]{0:T(1024)S(1)}, f32[768]{0:T(1024)}, u32[]{:S(2)}) copy-start(f32[768]{0:T(1024)} %get-tuple-element.658) | copy-start | bytes 9220
  609.7 21.6 %copy-start.39 = (f32[768]{0:T(1024)S(1)}, f32[768]{0:T(1024)}, u32[]{:S(2)}) copy-start(f32[768]{0:T(1024)} %get-tuple-element.599) | copy-start | bytes 9220
  609.7 22.9 %copy-start.38 = (f32[768]{0:T(1024)S(1)}, f32[768]{0:T(1024)}, u32[]{:S(2)}) copy-start(f32[768]{0:T(1024)} %get-tuple-element.603) | copy-start | bytes 9220
  (104 other events, 413.6 us)
Sparse Core Ops, SparseCore 0:
  12.8 46.6 all-gather.2
  62.2 42.9 all-gather.4
  1120.4 247.8 all-reduce.4
where the time goes:
time: 1440 us; the launch traced here: 1430 us
  blocking collectives  458 us (32%)
  waiting for transfers between devices  358 us (25%)
  local copies, waits for them, and re-layouts  299 us (21%)
  matrix products  131 us (9%)
  other arithmetic  106 us (7%)
  starting transfers between devices  58.3 us (4%)
    unnamed x1, blocking collectives  458 us
    unnamed x4, waiting for transfers between devices  243 us
    unnamed x123, local copies, waits for them, and re-layouts  133 us
    all_gather x1, waiting for transfers between devices, per_device(): v_all = lax.all_gather(v_flat, 'seq', axis=0, tiled=True)  45.8 us
    ppermute x16, starting transfers between devices, from_behind(): return lax.ppermute(shard, axis, pairs)  41.9 us
    all_gather x1, waiting for transfers between devices, per_device(): k_all = lax.all_gather(k_flat, 'seq', axis=0, tiled=True)  38.8 us
    slice x8, local copies, waits for them, and re-layouts, per_device(): outputs.append(whole[offset:offset + extent].reshape(member.shape))  35.9 us
    dot_general x16, matrix products, scores_of(): jnp.einsum('qhd,khd->hqk', q_heads, k_heads, preferred_element_type=jnp.f...  33.6 us
  transfers between devices with their start and end apart: 35, of which 19 were waited for; matrix products, arithmetic and copies ran while one was open for 9% of the time, Pallas kernels for 0%

commit v1 on v0

--- a/solution.py
+++ b/solution.py
@@ -130,8 +130,11 @@
         jnp.zeros((HEADS, rows, HD), jnp.float32),
     )
     state = start_state
-    k_all = lax.all_gather(k_flat, "seq", axis=0, tiled=True)
-    v_all = lax.all_gather(v_flat, "seq", axis=0, tiled=True)
+    k_all, v_all = jnp.split(
+        lax.all_gather(jnp.concatenate([k_flat, v_flat], axis=1), "seq", axis=0, tiled=True),
+        [k_flat.shape[1]],
+        axis=1,
+    )
     fold_extent = k_all.shape[0]
     number = fold_extent // rows
 

time: 1440 us -> 1420 us (0.986)
  waiting for transfers between devices: 358 us -> 325 us
    all_gather x2 -> x1, waiting for transfers between devices: 84.5 us -> 54 us  [per_device(): lax.all_gather(jnp.concatenate([k_flat, v_flat], axis=1), 'seq', axis=0,...]
    unnamed x123 -> x125, local copies, waits for them, and re-layouts: 133 us -> 134 us
    unnamed x4 -> x3, waiting for transfers between devices: 243 us -> 243 us
  transfers between devices with their start and end apart: 35 -> 34, of which waited for: 19 -> 18; matrix products, arithmetic and copies ran while one was open for 9% -> 9% of each run, Pallas kernels for 0% -> 0%
where the time goes in v1:
time: 1420 us; the launch traced here: 1410 us
  blocking collectives  458 us (32%)
  waiting for transfers between devices  325 us (23%)
  local copies, waits for them, and re-layouts  305 us (21%)
  matrix products  131 us (9%)
  other arithmetic  107 us (8%)
  starting transfers between devices  59.1 us (4%)
  between operations  14.6 us (1%)
    unnamed x1, blocking collectives  458 us
    unnamed x3, waiting for transfers between devices  243 us
    unnamed x125, local copies, waits for them, and re-layouts  134 us
    all_gather x1, waiting for transfers between devices, per_device(): lax.all_gather(jnp.concatenate([k_flat, v_flat], axis=1), 'seq', axis=0,...  54 us
    ppermute x16, starting transfers between devices, from_behind(): return lax.ppermute(shard, axis, pairs)  42.1 us
    slice x8, local copies, waits for them, and re-layouts, per_device(): outputs.append(whole[offset:offset + extent].reshape(member.shape))  35.9 us
    dot_general x16, matrix products, scores_of(): jnp.einsum('qhd,khd->hqk', q_heads, k_heads, preferred_element_type=jnp.f...  33.6 us
    while x152, local copies, waits for them, and re-layouts  31.6 us
  transfers between devices with their start and end apart: 34, of which 18 were waited for; matrix products, arithmetic and copies ran while one was open for 9% of the time, Pallas kernels for 0%

profile of v1, /device:TPU:0, one launch (start us, length us, event | category | flops | bytes accessed | tf_op | source)
XLA Modules:
  0.0 1405.8 jit_solution(11683303396505635094)
XLA Ops:
  22.7 54.0 %all-gather.2.cloned.1.call-done = bf16[1024,1536]{1,0:T(8,128)(2,1)} async-done(((bf16[128,1536]{1,0:T(8,128)(2,1)}), bf16[1024,1536]{1,0:T(8,128)(2,1)}) %all-gather.2.cloned.1.call-update) | async-done | bytes 3145744 | tf_op jit(solution)/shard_map/all_gather | solution.py:134
  76.7 3.7 fusion.70
  81.0 144.4 %while.39 = (s32[]{:T(128)}, f32[12,128]{1,0:T(8,128)}, f32[12,128]{1,0:T(8,128)}, f32[12,128,64]{1,2,0:T(8,128)}, s32[128]{0:T(128)}, /*index=5*/s32[9]{0:T(128...) while((s32[]{:T(128)}, f32[12,128]{1,0:T(8,128)}, ...), condition=%wide.region_8.9_spmd.clone, body=%wide.region_4.8_spmd.clone.sunk | while | flops 54422532 | bytes 5542175 | solution.py:148
  87.9 2.9 select_reduce_fusion.2
  105.2 2.9 select_reduce_fusion.2
  123.4 2.9 select_reduce_fusion.2
  141.5 2.9 select_reduce_fusion.2
  159.7 2.9 select_reduce_fusion.2
  177.8 2.9 select_reduce_fusion.2
  196.0 2.9 select_reduce_fusion.2
  214.2 2.9 select_reduce_fusion.2
  228.6 3.3 convolution_add_fusion.2
  232.0 5.5 convert_reduce_fusion.2
  247.6 215.2 %while.40 = (s32[]{:T(128)}, bf16[128,768]{0,1:T(8,128)(2,1)}, bf16[128,768]{0,1:T(8,128)(2,1)}, f32[128,768]{0,1:T(8,128)}, f32[128,768]{0,1:T(8,128)}, /*index...) while((s32[]{:T(128)}, bf16[128,768]{0,1:T(8,128)(2,1)}, ...), condition=%wide.region_15.16_spmd.clone, body=%wide.region_13.15_spmd.clone.sunk | while | flops 130993680 | bytes 19995340 | solution.py:211
  249.2 3.1 collective-permute-start
  254.0 4.3 collective-permute-start.1
  269.2 4.6 collective-permute-done.2
  282.9 3.2 collective-permute-start.1
  297.5 3.3 collective-permute-done.2
  309.8 3.7 collective-permute-start.1
  323.2 4.6 collective-permute-done.2
  362.1 3.2 collective-permute-start.1
  372.7 2.8 collective-permute-start.3
  389.0 3.7 collective-permute-start.1
  403.2 3.9 collective-permute-done.2
  441.4 3.2 collective-permute-start.1
  468.6 4.2 fusion.60
  475.0 5.3 convolution_bitcast_fusion.1
  480.3 5.2 fusion.51
  486.1 7.9 reshape.357
  496.3 9.6 copy.69
  506.0 10.8 reshape.360
  523.2 60.8 %dynamic-update-slice.3 = f32[7087872]{0:T(1024)} dynamic-update-slice(f32[7087872]{0:T(1024)} %constant_dynamic-update-slice_fusion.8, f32[1769472]{0:T(1024)} %reshape.357, s32[]{} %constant.149) | dynamic-update-slice | bytes 14155780
  585.3 20.3 %dynamic-update-slice.5 = f32[7087872]{0:T(1024)} dynamic-update-slice(f32[7087872]{0:T(1024)} %constant_dynamic-update-slice_fusion.7, f32[589824]{0:T(1024)S(1)} %reshape.358, s32[]{} %constant.151) | dynamic-update-slice | bytes 4718596
  609.5 9.3 constant_dynamic-update-slice_fusion.3
  619.4 3.9 constant_dynamic-update-slice_fusion.1
  623.9 457.8 %all-reduce.6 = bf16[7087872]{0:T(1024)(128)(2,1)} all-reduce(f32[7087872]{0:T(1024)} %constant_dynamic-update-slice_fusion), channel_id=2, replica_groups=mesh['seq'=8,'batch'=4] {'seq','batch'}, use_global_device_ids=true, to_apply=%region_26.27.clone | all-reduce | flops 7087872 | bytes 42527232
  1083.0 5.3 broadcast.252
  1088.2 7.6 dynamic-update-slice
  1097.2 4.1 fusion.35
  1101.3 242.7 %all-reduce.5.cloned.1.call-done = bf16[7087872]{0:T(1024)(128)(2,1)} async-done(((bf16[7087872]{0:T(1024)(128)(2,1)}), bf16[7087872]{0:T(1024)(128)(2,1)}) %all-reduce.5.cloned.1.call-update) | async-done | bytes 14175760
  1344.0 9.6 fusion.69
  1353.6 10.9 reshape.362
  1364.5 11.3 slice.81
  1375.7 4.6 slice.88
  1380.4 8.2 reshape.361
  1388.6 3.0 slice.90
  1391.7 3.4 slice.74
  (568 shorter events, 346.0 us)
Async XLA Ops:
  7.2 69.5 %all-gather.2.cloned.1.call-start = ((), (), s32[]{:S(2)}) async-start(), calls=%async_computation | async-start | bytes 3538944 | tf_op jit(solution)/shard_map/all_gather | solution.py:134
  13.4 1330.6 %all-reduce.5.cloned.1.call-start = ((), (), s32[]{:S(2)}) async-start(), calls=%async_computation.1 | async-start | bytes 28352512
  228.3 11.5 copy-start.4
  228.3 11.5 copy-start.37
  247.6 13.5 copy-start.49
  247.6 13.5 copy-start.50
  249.2 28.4 %collective-permute-start = (bf16[128,768]{0,1:T(8,128)(2,1)}, bf16[128,768]{0,1:T(8,128)(2,1)}, u32[]{:S(2)}, u32[]{:S(2)}) collective-permute-start(bf16[128,768]{0,1:T(8,128)(2,1)} %copy.93), channel_id=1, source_target_pairs={{0,4},{4,8},{8,12},{12,16},{16,20},{20,24},{24,28},{1,5},{5,9},{9,... | collective-permute-start | bytes 589832 | tf_op jit(solution)/shard_map/while/body/eval_jaxpr/ppermute | solution.py:16
  254.0 23.7 %collective-permute-start.1 = (bf16[128,768]{0,1:T(8,128)(2,1)}, bf16[128,768]{0,1:T(8,128)(2,1)}, u32[]{:S(2)}, u32[]{:S(2)}) collective-permute-start(bf16[128,768]{0,1:T(8,128)(2,1)} %copy.94), channel_id=1, source_target_pairs={{0,4},{4,8},{8,12},{12,16},{16,20},{20,24},{24,28},{1,5},{5,9},{9,... | collective-permute-start | bytes 589832 | tf_op jit(solution)/shard_map/while/body/eval_jaxpr/ppermute | solution.py:16
  263.9 10.0 collective-permute-start.2
  265.2 10.8 collective-permute-start.3
  279.3 25.2 %collective-permute-start = (bf16[128,768]{0,1:T(8,128)(2,1)}, bf16[128,768]{0,1:T(8,128)(2,1)}, u32[]{:S(2)}, u32[]{:S(2)}) collective-permute-start(bf16[128,768]{0,1:T(8,128)(2,1)} %copy.93), channel_id=1, source_target_pairs={{0,4},{4,8},{8,12},{12,16},{16,20},{20,24},{24,28},{1,5},{5,9},{9,... | collective-permute-start | bytes 589832 | tf_op jit(solution)/shard_map/while/body/eval_jaxpr/ppermute | solution.py:16
  282.9 21.7 %collective-permute-start.1 = (bf16[128,768]{0,1:T(8,128)(2,1)}, bf16[128,768]{0,1:T(8,128)(2,1)}, u32[]{:S(2)}, u32[]{:S(2)}) collective-permute-start(bf16[128,768]{0,1:T(8,128)(2,1)} %copy.94), channel_id=1, source_target_pairs={{0,4},{4,8},{8,12},{12,16},{16,20},{20,24},{24,28},{1,5},{5,9},{9,... | collective-permute-start | bytes 589832 | tf_op jit(solution)/shard_map/while/body/eval_jaxpr/ppermute | solution.py:16
  291.7 9.0 collective-permute-start.2
  293.0 9.8 collective-permute-start.3
  304.6 11.7 copy-start.49
  304.6 11.7 copy-start.50
  306.2 25.4 %collective-permute-start = (bf16[128,768]{0,1:T(8,128)(2,1)}, bf16[128,768]{0,1:T(8,128)(2,1)}, u32[]{:S(2)}, u32[]{:S(2)}) collective-permute-start(bf16[128,768]{0,1:T(8,128)(2,1)} %copy.93), channel_id=1, source_target_pairs={{0,4},{4,8},{8,12},{12,16},{16,20},{20,24},{24,28},{1,5},{5,9},{9,... | collective-permute-start | bytes 589832 | tf_op jit(solution)/shard_map/while/body/eval_jaxpr/ppermute | solution.py:16
  309.8 21.8 %collective-permute-start.1 = (bf16[128,768]{0,1:T(8,128)(2,1)}, bf16[128,768]{0,1:T(8,128)(2,1)}, u32[]{:S(2)}, u32[]{:S(2)}) collective-permute-start(bf16[128,768]{0,1:T(8,128)(2,1)} %copy.94), channel_id=1, source_target_pairs={{0,4},{4,8},{8,12},{12,16},{16,20},{20,24},{24,28},{1,5},{5,9},{9,... | collective-permute-start | bytes 589832 | tf_op jit(solution)/shard_map/while/body/eval_jaxpr/ppermute | solution.py:16
  319.1 8.7 collective-permute-start.2
  320.4 9.5 collective-permute-start.3
  333.2 23.7 %collective-permute-start = (bf16[128,768]{0,1:T(8,128)(2,1)}, bf16[128,768]{0,1:T(8,128)(2,1)}, u32[]{:S(2)}, u32[]{:S(2)}) collective-permute-start(bf16[128,768]{0,1:T(8,128)(2,1)} %copy.93), channel_id=1, source_target_pairs={{0,4},{4,8},{8,12},{12,16},{16,20},{20,24},{24,28},{1,5},{5,9},{9,... | collective-permute-start | bytes 589832 | tf_op jit(solution)/shard_map/while/body/eval_jaxpr/ppermute | solution.py:16
  336.8 20.1 %collective-permute-start.1 = (bf16[128,768]{0,1:T(8,128)(2,1)}, bf16[128,768]{0,1:T(8,128)(2,1)}, u32[]{:S(2)}, u32[]{:S(2)}) collective-permute-start(bf16[128,768]{0,1:T(8,128)(2,1)} %copy.94), channel_id=1, source_target_pairs={{0,4},{4,8},{8,12},{12,16},{16,20},{20,24},{24,28},{1,5},{5,9},{9,... | collective-permute-start | bytes 589832 | tf_op jit(solution)/shard_map/while/body/eval_jaxpr/ppermute | solution.py:16
  344.4 8.7 collective-permute-start.2
  345.7 9.5 collective-permute-start.3
  356.9 11.3 copy-start.50
  358.6 24.9 %collective-permute-start = (bf16[128,768]{0,1:T(8,128)(2,1)}, bf16[128,768]{0,1:T(8,128)(2,1)}, u32[]{:S(2)}, u32[]{:S(2)}) collective-permute-start(bf16[128,768]{0,1:T(8,128)(2,1)} %copy.93), channel_id=1, source_target_pairs={{0,4},{4,8},{8,12},{12,16},{16,20},{20,24},{24,28},{1,5},{5,9},{9,... | collective-permute-start | bytes 589832 | tf_op jit(solution)/shard_map/while/body/eval_jaxpr/ppermute | solution.py:16
  362.1 21.4 %collective-permute-start.1 = (bf16[128,768]{0,1:T(8,128)(2,1)}, bf16[128,768]{0,1:T(8,128)(2,1)}, u32[]{:S(2)}, u32[]{:S(2)}) collective-permute-start(bf16[128,768]{0,1:T(8,128)(2,1)} %copy.94), channel_id=1, source_target_pairs={{0,4},{4,8},{8,12},{12,16},{16,20},{20,24},{24,28},{1,5},{5,9},{9,... | collective-permute-start | bytes 589832 | tf_op jit(solution)/shard_map/while/body/eval_jaxpr/ppermute | solution.py:16
  371.0 8.7 collective-permute-start.2
  372.7 9.1 collective-permute-start.3
  383.5 12.1 copy-start.49
  383.5 12.1 copy-start.50
  385.1 25.7 %collective-permute-start = (bf16[128,768]{0,1:T(8,128)(2,1)}, bf16[128,768]{0,1:T(8,128)(2,1)}, u32[]{:S(2)}, u32[]{:S(2)}) collective-permute-start(bf16[128,768]{0,1:T(8,128)(2,1)} %copy.93), channel_id=1, source_target_pairs={{0,4},{4,8},{8,12},{12,16},{16,20},{20,24},{24,28},{1,5},{5,9},{9,... | collective-permute-start | bytes 589832 | tf_op jit(solution)/shard_map/while/body/eval_jaxpr/ppermute | solution.py:16
  389.0 21.8 %collective-permute-start.1 = (bf16[128,768]{0,1:T(8,128)(2,1)}, bf16[128,768]{0,1:T(8,128)(2,1)}, u32[]{:S(2)}, u32[]{:S(2)}) collective-permute-start(bf16[128,768]{0,1:T(8,128)(2,1)} %copy.94), channel_id=1, source_target_pairs={{0,4},{4,8},{8,12},{12,16},{16,20},{20,24},{24,28},{1,5},{5,9},{9,... | collective-permute-start | bytes 589832 | tf_op jit(solution)/shard_map/while/body/eval_jaxpr/ppermute | solution.py:16
  398.4 8.7 collective-permute-start.2
  399.7 9.5 collective-permute-start.3
  412.5 23.7 %collective-permute-start = (bf16[128,768]{0,1:T(8,128)(2,1)}, bf16[128,768]{0,1:T(8,128)(2,1)}, u32[]{:S(2)}, u32[]{:S(2)}) collective-permute-start(bf16[128,768]{0,1:T(8,128)(2,1)} %copy.93), channel_id=1, source_target_pairs={{0,4},{4,8},{8,12},{12,16},{16,20},{20,24},{24,28},{1,5},{5,9},{9,... | collective-permute-start | bytes 589832 | tf_op jit(solution)/shard_map/while/body/eval_jaxpr/ppermute | solution.py:16
  416.1 20.1 %collective-permute-start.1 = (bf16[128,768]{0,1:T(8,128)(2,1)}, bf16[128,768]{0,1:T(8,128)(2,1)}, u32[]{:S(2)}, u32[]{:S(2)}) collective-permute-start(bf16[128,768]{0,1:T(8,128)(2,1)} %copy.94), channel_id=1, source_target_pairs={{0,4},{4,8},{8,12},{12,16},{16,20},{20,24},{24,28},{1,5},{5,9},{9,... | collective-permute-start | bytes 589832 | tf_op jit(solution)/shard_map/while/body/eval_jaxpr/ppermute | solution.py:16
  423.7 8.7 collective-permute-start.2
  425.0 9.5 collective-permute-start.3
  436.2 11.3 copy-start.50
  437.8 24.9 %collective-permute-start = (bf16[128,768]{0,1:T(8,128)(2,1)}, bf16[128,768]{0,1:T(8,128)(2,1)}, u32[]{:S(2)}, u32[]{:S(2)}) collective-permute-start(bf16[128,768]{0,1:T(8,128)(2,1)} %copy.93), channel_id=1, source_target_pairs={{0,4},{4,8},{8,12},{12,16},{16,20},{20,24},{24,28},{1,5},{5,9},{9,... | collective-permute-start | bytes 589832 | tf_op jit(solution)/shard_map/while/body/eval_jaxpr/ppermute | solution.py:16
  441.4 21.4 %collective-permute-start.1 = (bf16[128,768]{0,1:T(8,128)(2,1)}, bf16[128,768]{0,1:T(8,128)(2,1)}, u32[]{:S(2)}, u32[]{:S(2)}) collective-permute-start(bf16[128,768]{0,1:T(8,128)(2,1)} %copy.94), channel_id=1, source_target_pairs={{0,4},{4,8},{8,12},{12,16},{16,20},{20,24},{24,28},{1,5},{5,9},{9,... | collective-permute-start | bytes 589832 | tf_op jit(solution)/shard_map/while/body/eval_jaxpr/ppermute | solution.py:16
  450.3 8.7 collective-permute-start.2
  451.9 9.1 collective-permute-start.3
  506.0 12.1 copy-start.16
  585.3 20.3 %copy-start.41 = (f32[768]{0:T(1024)S(1)}, f32[768]{0:T(1024)}, u32[]{:S(2)}) copy-start(f32[768]{0:T(1024)} %get-tuple-element.658) | copy-start | bytes 9220
  585.3 21.6 %copy-start.40 = (f32[768]{0:T(1024)S(1)}, f32[768]{0:T(1024)}, u32[]{:S(2)}) copy-start(f32[768]{0:T(1024)} %get-tuple-element.599) | copy-start | bytes 9220
  585.3 22.9 %copy-start.39 = (f32[768]{0:T(1024)S(1)}, f32[768]{0:T(1024)}, u32[]{:S(2)}) copy-start(f32[768]{0:T(1024)} %get-tuple-element.603) | copy-start | bytes 9220
  (104 other events, 404.2 us)
Sparse Core Ops, SparseCore 0:
  13.5 63.1 all-gather.1
  1096.0 247.9 all-reduce.4
